TPU v7x, 32 devices: a whole 2x2x4 slice. The times are simulated.
32 devices in a mesh: section: 8 (over z, x), expert: 4 (over y, core).
Axes of the slice: x: 2, y: 2, z: 4, core: 2. Of those that a mesh axis runs over, the one named last changes fastest.
Arguments:
- tokens: bfloat16 [128, 6144], P('section', 'expert'), may hold values from -6 to 6
- gains: float32 [6144], replicated, may hold values from 0.1 to 1.9
- w_gate: bfloat16 [4, 6144, 2048], P('expert', None, 'section'), may hold values from -0.078125 to 0.078125
- w_up: bfloat16 [4, 6144, 2048], P('expert', None, 'section'), may hold values from -0.078125 to 0.078125
- w_down: bfloat16 [4, 2048, 6144], P('expert', 'section'), may hold values from -0.125 to 0.125
- expert_ids: int32 [128, 2], replicated, may hold values from 0 to 3, all different within a row; in each aligned block of 16 rows (0 to 15, 16 to 31, ...) at most 12 rows name the same one
- gate_ints: int32 [128, 2], replicated, may hold values from 1 to 65535
Outputs:
- mixed: bfloat16 [128, 6144], P('section', 'expert')
Inputs may be any that keep to these rules, and one draw needn't show every extreme that they name: `expert_ids`: in each aligned block of 16 token rows (the rows of one index of section), no expert is named by more than 12 rows.
All inputs are finite; a program needn't handle non-finite values.
Results may differ from a plain program's by a relative error of at most 0.0042.
Values may be sent and summed in bfloat16 or wider, within the bound.
A program may use at most 128 MiB of HBM per device.

v0:
```python
import jax
import jax.numpy as jnp
from jax import lax
from jax.sharding import PartitionSpec as P

TOP = 2
CAP = 12


def expert_product(rows, gate_w, up_w, down_w):
    gate_val = jnp.dot(rows, gate_w, preferred_element_type=jnp.float32)
    up_val = jnp.dot(rows, up_w, preferred_element_type=jnp.float32)
    hidden_act = (jax.nn.silu(gate_val) * up_val).astype(jnp.bfloat16)
    return jnp.dot(hidden_act, down_w, preferred_element_type=jnp.float32)


def body(tokens, gains, w_gate, w_up, w_down, expert_ids, gate_ints):
    expert = lax.axis_index("expert")
    own_section = lax.axis_index("section")
    full_rows = lax.all_gather(tokens, "expert", axis=1, tiled=True)
    tok_rows = full_rows.shape[0]
    floated = full_rows.astype(jnp.float32)
    mean_sq = jnp.mean(floated * floated, axis=-1, keepdims=True)
    normed = (floated * lax.rsqrt(mean_sq + 1e-05) * gains).astype(jnp.bfloat16)
    shards = expert_ids.shape[0] // tok_rows
    route_ids = expert_ids.reshape((shards, tok_rows, TOP))
    route_ints = gate_ints.reshape((shards, tok_rows, TOP))
    chosen = route_ids == expert
    weight = jnp.sum(jnp.where(chosen, route_ints.astype(jnp.float32) / 65536.0, 0.0), axis=-1)
    selected = jnp.any(chosen, axis=-1)
    places = jnp.cumsum(selected.astype(jnp.int32), axis=1) - 1
    slot_of = jnp.clip(places, 0, CAP - 1)
    own_selected = lax.dynamic_index_in_dim(selected, own_section, 0, keepdims=False)
    own_places = lax.dynamic_index_in_dim(places, own_section, 0, keepdims=False)
    slot_match = (own_places[None, :] == jnp.arange(CAP, dtype=jnp.int32)[:, None]) & own_selected[
        None, :
    ]
    picked = jnp.dot(
        slot_match.astype(jnp.bfloat16), normed, preferred_element_type=jnp.float32
    ).astype(jnp.bfloat16)
    gate_w = w_gate[0]
    up_w = w_up[0]
    down_w = w_down[0]
    routed = lax.all_gather(picked, "section", axis=0, tiled=True)
    partial_value = expert_product(routed, gate_w, up_w, down_w)
    own_rows = lax.psum_scatter(partial_value, "section", scatter_dimension=0, tiled=True)
    own_slots = lax.dynamic_index_in_dim(slot_of, own_section, 0, keepdims=False)
    own_weight = lax.dynamic_index_in_dim(weight, own_section, 0, keepdims=False)
    token_term = own_rows[own_slots] * own_weight[:, None]
    summed = lax.psum_scatter(token_term, "expert", scatter_dimension=1, tiled=True)
    return (tokens.astype(jnp.float32) + summed).astype(jnp.bfloat16)


def solution(mesh):
    in_specs = (
        P("section", "expert"),
        P(),
        P("expert", None, "section"),
        P("expert", None, "section"),
        P("expert", "section", None),
        P(),
        P(),
    )
    out_specs = P("section", "expert")
    return jax.shard_map(body, mesh=mesh, in_specs=in_specs, out_specs=out_specs, check_vma=False)
```

profile of v0, /device:TPU:0, one launch (start us, length us, event | category | flops | bytes accessed | tf_op | source)
XLA Modules:
  0.0 206.6 jit_solution(13355044070359625755)
XLA Ops:
  6.5 0.0 copy-start
  6.5 0.0 all-gather.3.cloned.1.call-start
  6.5 0.8 fusion.37
  7.4 0.1 reduce_or.12
  7.5 0.2 reduce_window_sum.11
  7.7 7.1 %all_gather.6 = bf16[16,6144]{1,0:T(8,128)(2,1)S(1)} all-gather(bf16[16,1536]{1,0:T(8,128)(2,1)} %param.7), channel_id=1, replica_groups=mesh['section'=8,'expert'=4] {'expert'}, dimensions={1}, use_global_device_ids=true | all-gather | bytes 245760 | tf_op jit(solution)/shard_map/all_gather | solution.py:20
  14.8 0.2 fusion.16
  14.9 1.7 fusion.1
  16.6 0.0 all-gather.3.cloned.1.call-update
  16.6 0.0 reduce-scatter.4.cloned.1.call-start
  16.7 45.7 %all-gather.3.cloned.1.call-done = bf16[8,12,6144]{2,1,0:T(8,128)(2,1)} async-done(((bf16[1,12,6144]{2,1,0:T(8,128)(2,1)}), bf16[8,12,6144]{2,1,0:T(8,128)(2,1)}) %all-gather.3.cloned.1.call-update) | async-done | bytes 1179664 | tf_op jit(solution)/shard_map/all_gather | solution.py:44
  62.4 2.3 %reshape.52 = bf16[96,6144]{1,0:T(8,128)(2,1)} reshape(bf16[8,12,6144]{2,1,0:T(8,128)(2,1)} %all-gather.3.cloned.1.call-done) | data formatting | bytes 2359296
  64.8 2.9 %fusion.6 = f32[96,256]{1,0:T(8,128)S(1)} fusion(bf16[96,6144]{1,0:T(8,128)(2,1)} %reshape.52, bf16[1,6144,256]{2,1,0:T(8,128)(2,1)} %param.9), kind=kOutput, calls=%fused_computation.7 | convolution fusion | flops 301989888 | bytes 4423680 | tf_op jit(solution)/shard_map/dot_general | solution.py:11
  67.7 0.0 copy-done
  67.7 0.0 copy-start.1
  67.7 0.0 copy-start.2
  67.7 5.5 %fusion.2 = f32[96,6144]{1,0:T(8,128)} fusion(bf16[1,256,6144]{2,1,0:T(8,128)(2,1)S(1)} %copy-done, bf16[96,6144]{1,0:T(8,128)(2,1)} %reshape.52, bf16[1,6144,256]{2,1,0:T(8,128)(2,1)} %param.10, f32[96,256]{1,0:T(8,128)S(1)} %fusion.6), kind=kOutput, calls=%fused_computation.3 | convolution fusion | flops 604127232 | bytes 9928704 | tf_op jit(solution)/shard_map/dot_general | solution.py:14
  73.2 70.4 %fusion = f32[16,6144]{1,0:T(8,128)S(1)} fusion(f32[96,6144]{1,0:T(8,128)} %fusion.2), kind=kCustom, calls=%all-reduce-scatter | all-reduce-scatter fusion | flops 786433 | bytes 2753024
  143.7 2.0 collective-permute-start
  145.7 0.0 copy-done.1
  145.7 0.0 copy-done.2
  145.7 0.1 reduce_sum.22
  145.8 1.2 dynamic-slice.4
  147.8 4.5 %collective-permute-start.1 = (f32[12,6144]{1,0:T(8,128)S(1)}, f32[12,6144]{1,0:T(8,128)}, u32[]{:S(2)}, u32[]{:S(2)}) collective-permute-start(f32[12,6144]{1,0:T(8,128)S(1)} %slice.2), channel_id=1, source_target_pairs={{0,8},{4,12},{8,16},{12,20},{16,24},{20,28},{1,9},{5,13},{9,17},{1... | collective-permute-start | bytes 884744
  152.2 6.2 %collective-permute-done.1 = f32[12,6144]{1,0:T(8,128)} collective-permute-done((f32[12,6144]{1,0:T(8,128)S(1)}, f32[12,6144]{1,0:T(8,128)}, u32[]{:S(2)}, u32[]{:S(2)}) %collective-permute-start.1) | collective-permute-done | bytes 294944
  158.4 0.0 collective-permute-done
  158.4 10.1 %concatenate = f32[44,6144]{1,0:T(8,128)} concatenate(f32[12,6144]{1,0:T(8,128)} %collective-permute-done.1, f32[16,6144]{1,0:T(8,128)} %collective-permute-done, f32[16,6144]{1,0:T(8,128)S(1)} %fusion), dimensions={0} | concatenate | bytes 2162688
  168.6 1.1 constant_dynamic-slice_fusion
  169.7 1.4 gather_fusion
  171.1 1.8 broadcast_multiply_fusion
  172.9 0.0 reduce-scatter.4.cloned.1.call-update
  172.9 25.3 %reduce-scatter.4.cloned.1.call-done = f32[16,1536]{1,0:T(8,128)} async-done(((f32[16,6144]{1,0:T(8,128)}), f32[16,1536]{1,0:T(8,128)}) %reduce-scatter.4.cloned.1.call-update) | async-done | bytes 98320 | tf_op jit(solution)/shard_map/reduce_scatter | solution.py:50
  198.2 1.5 add_convert_fusion
  (10 shorter events, 0.1 us)
Async XLA Ops:
  6.5 61.1 %copy-start = (bf16[1,256,6144]{2,1,0:T(8,128)(2,1)S(1)}, bf16[1,256,6144]{2,1,0:T(8,128)(2,1)}, u32[]{:S(2)}) copy-start(bf16[1,256,6144]{2,1,0:T(8,128)(2,1)} %param.11) | copy-start | bytes 9437188
  6.5 55.9 %all-gather.3.cloned.1.call-start = ((), (), s32[]{:S(2)}) async-start(), calls=%async_computation.2 | async-start | bytes 1769472 | tf_op jit(solution)/shard_map/all_gather | solution.py:44
  16.6 181.6 %reduce-scatter.4.cloned.1.call-start = ((), (), s32[]{:S(2)}) async-start(), calls=%async_computation.1 | async-start | bytes 491520 | tf_op jit(solution)/shard_map/reduce_scatter | solution.py:50
  67.7 78.0 %copy-start.1 = (s32[128,2]{0,1:T(2,128)S(1)}, s32[128,2]{0,1:T(2,128)}, u32[]{:S(2)}) copy-start(s32[128,2]{0,1:T(2,128)} %param.12) | copy-start | bytes 3076
  67.7 78.0 %copy-start.2 = (s32[128,2]{0,1:T(2,128)S(1)}, s32[128,2]{0,1:T(2,128)}, u32[]{:S(2)}) copy-start(s32[128,2]{0,1:T(2,128)} %param.13) | copy-start | bytes 3076
  143.7 14.8 %collective-permute-start = (f32[16,6144]{1,0:T(8,128)S(1)}, f32[16,6144]{1,0:T(8,128)}, u32[]{:S(2)}, u32[]{:S(2)}) collective-permute-start(f32[16,6144]{1,0:T(8,128)S(1)} %fusion), channel_id=1, source_target_pairs={{0,4},{4,8},{8,12},{12,16},{16,20},{20,24},{24,28},{1,5},{5,9},{9,... | collective-permute-start | bytes 1179656
  147.8 10.7 %collective-permute-start.1 = (f32[12,6144]{1,0:T(8,128)S(1)}, f32[12,6144]{1,0:T(8,128)}, u32[]{:S(2)}, u32[]{:S(2)}) collective-permute-start(f32[12,6144]{1,0:T(8,128)S(1)} %slice.2), channel_id=1, source_target_pairs={{0,8},{4,12},{8,16},{12,20},{16,24},{20,28},{1,9},{5,13},{9,17},{1... | collective-permute-start | bytes 884744
Sparse Core Ops, SparseCore 0:
  16.8 45.6 all-gather.2
  173.0 25.1 reduce-scatter.3
where the time goes:
time: 207 us
  blocking collectives  77.5 us (37%)
  waiting for transfers between devices  77.3 us (37%)
  local copies, waits for them, and re-layouts  16.4 us (8%)
  between operations  14.1 us (7%)
  matrix products  10.1 us (5%)
  starting transfers between devices  6.54 us (3%)
  other arithmetic  4.59 us (2%)
    unnamed x1, blocking collectives  70.4 us
    all_gather x1, waiting for transfers between devices, body(): routed = lax.all_gather(picked, 'section', axis=0, tiled=True)  45.7 us
    reduce_scatter x1, waiting for transfers between devices, body(): lax.psum_scatter(token_term, 'expert', scatter_dimension=1, tiled=True)  25.3 us
    unnamed x11, local copies, waits for them, and re-layouts  14.8 us
    all_gather x1, blocking collectives, body(): full_rows = lax.all_gather(tokens, 'expert', axis=1, tiled=True)  7.08 us
    unnamed x2, starting transfers between devices  6.5 us
    unnamed x4, waiting for transfers between devices  6.22 us
    dot_general x1, matrix products, expert_product(): return jnp.dot(hidden_act, down_w, preferred_element_type=jnp.float32)  5.53 us
  transfers between devices with their start and end apart: 4, of which 3 were waited for; matrix products, arithmetic and copies ran while one was open for 1% of the time, Pallas kernels for 0%

commit v1 on v0

v1 whole, which is shorter than its diff:
```python
import functools

import jax
import jax.numpy as jnp
from jax import lax
from jax.experimental import pallas as pl
from jax.experimental.pallas import tpu as pltpu
from jax.sharding import PartitionSpec as P

EPS = 1e-05
MESH = pl.DeviceIdType.MESH
BF16 = jnp.bfloat16
F32 = jnp.float32
TILE = 128


def flip(index, mask):
    bit = 1
    while bit <= mask:
        if mask & bit:
            index = index + bit - 2 * bit * lax.rem(lax.div(index, bit), 2)
        bit *= 2
    return index


def kernel(
    depth, tok, gains, wg, wu, wd, ids, ints, out,
    x, xn, w_in, w_out, gains_v, ids_v, ints_v, inner, weight,
    own, sib_s, sib_r, b_s, b_r, a_s, a_r, z_s, z_r,
    load_sem, in_recv, in_sib_recv, in_z_send, in_a_send, in_b_send, in_sib_send,
    sib_send, sib_recv, b_send, b_recv, a_send, a_recv, z_send, z_recv,
):
    section, expert = lax.axis_index("section"), lax.axis_index("expert")
    z, px = lax.div(section, 2), lax.rem(section, 2)
    py, core = lax.div(expert, 2), lax.rem(expert, 2)
    rows, width = tok.shape
    total = x.shape[1]
    hid = wg.shape[2]
    features = x.shape[0] * width
    i = py * (1 - core) + px * core
    j = px * (1 - core) + py * core

    def place(zz, ii, jj):
        yy = ii * (1 - core) + jj * core
        xx = jj * (1 - core) + ii * core
        return zz * 2 + xx, yy

    def rows_of(sec):
        return pl.ds(pl.multiple_of(sec * rows, rows), rows)

    def device(zz, ii, jj):
        sec, yy = place(zz, ii, jj)
        return sec, yy * 2 + core

    a_dev = device(z, i, 1 - j)
    b_dev = device(z, 1 - i, j)
    sib_dev = (section, py * 2 + 1 - core)
    z_devs = [(flip(z, k) * 2 + px, expert) for k in range(1, depth)]

    loads = [
        pltpu.make_async_copy(tok, x.at[expert, rows_of(section)], load_sem.at[0]),
        pltpu.make_async_copy(wg.at[0], w_in.at[:, pl.ds(0, hid)], load_sem.at[1]),
        pltpu.make_async_copy(wu.at[0], w_in.at[:, pl.ds(hid, hid)], load_sem.at[2]),
        pltpu.make_async_copy(gains, gains_v, load_sem.at[3]),
        pltpu.make_async_copy(ids, ids_v, load_sem.at[4]),
        pltpu.make_async_copy(ints, ints_v, load_sem.at[5]),
    ] + [
        pltpu.make_async_copy(
            wd.at[0, :, pl.ds(e * width, width)], w_out.at[e], load_sem.at[6 + e]
        )
        for e in range(x.shape[0])
    ]
    for load in loads:
        load.start()

    barrier = pltpu.get_barrier_semaphore()
    partners = z_devs + [a_dev, b_dev, sib_dev]
    for partner in partners:
        pl.semaphore_signal(barrier, inc=1, device_id=partner, device_id_type=MESH)
    pl.semaphore_wait(barrier, len(partners))

    pending = []

    def block(zz, ii, jj):
        sec, yy = place(zz, ii, jj)
        return x.at[yy * 2 + core, rows_of(sec)]

    def push(source, zz, ii, jj, send_sem, target):
        copy = pltpu.make_async_remote_copy(
            src_ref=source, dst_ref=block(zz, ii, jj), send_sem=send_sem,
            recv_sem=in_recv.at[(zz * 2 + ii) * 2 + jj],
            device_id=target, device_id_type=MESH,
        )
        copy.start()
        pending.append(copy)

    def push_sib(source, zz, ii, jj):
        sec, yy = place(zz, ii, jj)
        copy = pltpu.make_async_remote_copy(
            src_ref=source, dst_ref=block(zz, ii, jj), send_sem=in_sib_send.at[sec * 2 + yy],
            recv_sem=in_sib_recv.at[sec * 2 + yy],
            device_id=sib_dev, device_id_type=MESH,
        )
        copy.start()
        pending.append(copy)

    def arrived(zz, ii, jj):
        here = block(zz, ii, jj)
        pltpu.make_async_remote_copy(
            src_ref=here, dst_ref=here, send_sem=in_z_send.at[0],
            recv_sem=in_recv.at[(zz * 2 + ii) * 2 + jj],
            device_id=sib_dev, device_id_type=MESH,
        ).wait_recv()
        return here

    for k in range(1, depth):
        push(tok, z, i, j, in_z_send.at[k - 1], z_devs[k - 1])
    push(tok, z, i, j, in_a_send.at[0], a_dev)
    push(tok, z, i, j, in_b_send.at[0], b_dev)
    push_sib(tok, z, i, j)
    for k in range(1, depth):
        zz = flip(z, k)
        here = arrived(zz, i, j)
        push(here, zz, i, j, in_a_send.at[k], a_dev)
        push(here, zz, i, j, in_b_send.at[k], b_dev)
        push_sib(here, zz, i, j)
    for k in range(depth):
        zz = flip(z, k)
        here = arrived(zz, i, 1 - j)
        push(here, zz, i, 1 - j, in_b_send.at[depth + k], b_dev)
        push_sib(here, zz, i, 1 - j)
    for jj in (j, 1 - j):
        for k in range(depth):
            zz = flip(z, k)
            push_sib(arrived(zz, 1 - i, jj), zz, 1 - i, jj)

    for load in loads:
        load.wait()
    chosen = jnp.where(ids_v[...] == expert, ints_v[...].astype(F32) / 65536.0, 0.0)
    row = jnp.sum(chosen, axis=0, keepdims=True)
    weight[...] = jnp.broadcast_to(row, (8, total)).T[:, :1]

    for sec in range(2 * depth):
        for yy in range(2):
            here = x.at[yy * 2 + 1 - core, rows_of(sec)]
            pltpu.make_async_remote_copy(
                src_ref=here, dst_ref=here, send_sem=in_z_send.at[0],
                recv_sem=in_sib_recv.at[sec * 2 + yy],
                device_id=sib_dev, device_id_type=MESH,
            ).wait_recv()

    slices = range(x.shape[0])

    def tiles(body):
        if total == TILE:
            body(pl.ds(0, TILE))
        else:
            @pl.loop(0, total // TILE)
            def _(t):
                body(pl.ds(pl.multiple_of(t * TILE, TILE), TILE))

    def hidden(span):
        squares = 0.0
        for e in slices:
            part = x[e, span].astype(F32)
            squares = squares + jnp.sum(part * part, axis=-1, keepdims=True)
        scale = lax.rsqrt(squares / features + EPS)
        both = jnp.zeros((TILE, 2 * hid), F32)
        for e in slices:
            cols = pl.ds(e * width, width)
            xn[e] = (x[e, span].astype(F32) * scale * gains_v[:, cols]).astype(BF16)
            both = both + jnp.dot(xn[e], w_in[cols], preferred_element_type=F32)
        gate, up = both[:, :hid], both[:, hid:]
        inner[span] = (gate / (1.0 + jnp.exp(-gate)) * up).astype(BF16)

    tiles(hidden)

    def down(e, target, kind):
        def one(span):
            target[span] = (
                jnp.dot(inner[span], w_out[e], preferred_element_type=F32) * weight[span]
            ).astype(kind)
        tiles(one)

    for n, yy in enumerate((1 - py, py)):
        down(yy * 2 + 1 - core, sib_s.at[yy], BF16)
        copy = pltpu.make_async_remote_copy(
            src_ref=sib_s.at[yy], dst_ref=sib_r.at[yy], send_sem=sib_send.at[yy],
            recv_sem=sib_recv.at[yy], device_id=sib_dev, device_id_type=MESH,
        )
        copy.start()
        pending.append(copy)
    for yy in (1 - py, py):
        down(yy * 2 + core, own.at[yy], F32)
    for yy in (1 - py, py):
        pltpu.make_async_remote_copy(
            src_ref=sib_s.at[yy], dst_ref=sib_r.at[yy], send_sem=sib_send.at[yy],
            recv_sem=sib_recv.at[yy], device_id=sib_dev, device_id_type=MESH,
        ).wait_recv()

    def pair(zz, ii, jj):
        sec, yy = place(zz, ii, jj)
        span = rows_of(sec)
        return own[yy, span] + sib_r[yy, span].astype(F32)

    def send(value, source, source_slot, target, target_slot, send_sem, recv_sem, dev):
        source[source_slot] = value.astype(BF16)
        copy = pltpu.make_async_remote_copy(
            src_ref=source.at[source_slot], dst_ref=target.at[target_slot],
            send_sem=send_sem.at[source_slot], recv_sem=recv_sem.at[target_slot],
            device_id=dev, device_id_type=MESH,
        )
        copy.start()
        pending.append(copy)

    def take(target, slot, recv_sem):
        pltpu.make_async_remote_copy(
            src_ref=target.at[slot], dst_ref=target.at[slot], send_sem=in_z_send.at[0],
            recv_sem=recv_sem.at[slot], device_id=sib_dev, device_id_type=MESH,
        ).wait_recv()
        return target[slot].astype(F32)

    order = list(range(1, depth)) + [0]
    for jj in (1 - j, j):
        for k in order:
            zz = flip(z, k)
            slot = jj * depth + zz
            send(pair(zz, 1 - i, jj), b_s, slot, b_r, slot, b_send, b_recv, b_dev)
    for k in order:
        zz = flip(z, k)
        value = pair(zz, i, 1 - j) + take(b_r, (1 - j) * depth + zz, b_recv)
        send(value, a_s, zz, a_r, zz, a_send, a_recv, a_dev)
    for k in order:
        zz = flip(z, k)
        value = pair(zz, i, j) + take(b_r, j * depth + zz, b_recv) + take(a_r, zz, a_recv)
        if k:
            send(value, z_s, zz, z_r, z, z_send, z_recv, z_devs[k - 1])
    for k in range(1, depth):
        value = value + take(z_r, flip(z, k), z_recv)
    out[...] = (x[expert, rows_of(section)].astype(F32) + value).astype(BF16)
    for copy in pending:
        copy.wait_send()


def body(tokens, gains, w_gate, w_up, w_down, expert_ids, gate_ints, *, sections, experts):
    rows, width = tokens.shape
    hid = w_gate.shape[2]
    features = gains.shape[0]
    total = expert_ids.shape[0]
    top = expert_ids.shape[1]
    depth = sections // 2
    dma = pltpu.SemaphoreType.DMA
    blocks = 4 * depth
    return pl.pallas_call(
        functools.partial(kernel, depth),
        out_shape=jax.ShapeDtypeStruct((rows, width), BF16),
        in_specs=[pl.BlockSpec(memory_space=pl.ANY)] * 7,
        out_specs=pl.BlockSpec(memory_space=pltpu.VMEM),
        scratch_shapes=[
            pltpu.VMEM((experts, total, width), BF16),
            pltpu.VMEM((experts, TILE, width), BF16),
            pltpu.VMEM((features, 2 * hid), BF16),
            pltpu.VMEM((experts, hid, width), BF16),
            pltpu.VMEM((1, features), F32),
            pltpu.VMEM((top, total), jnp.int32),
            pltpu.VMEM((top, total), jnp.int32),
            pltpu.VMEM((total, hid), BF16),
            pltpu.VMEM((total, 1), F32),
            pltpu.VMEM((2, total, width), F32),
            pltpu.VMEM((2, total, width), BF16),
            pltpu.VMEM((2, total, width), BF16),
            pltpu.VMEM((2 * depth, rows, width), BF16),
            pltpu.VMEM((2 * depth, rows, width), BF16),
            pltpu.VMEM((depth, rows, width), BF16),
            pltpu.VMEM((depth, rows, width), BF16),
            pltpu.VMEM((depth, rows, width), BF16),
            pltpu.VMEM((depth, rows, width), BF16),
            dma((6 + experts,)),
            dma((blocks,)), dma((blocks,)),
            dma((depth,)), dma((depth,)), dma((2 * depth,)), dma((blocks,)),
            dma((2,)), dma((2,)),
            dma((2 * depth,)), dma((2 * depth,)),
            dma((depth,)), dma((depth,)),
            dma((depth,)), dma((depth,)),
        ],
        compiler_params=pltpu.CompilerParams(
            collective_id=0, has_side_effects=True, vmem_limit_bytes=62 * 1024 * 1024,
        ),
    )(tokens, gains.reshape(1, features), w_gate, w_up, w_down, expert_ids.T, gate_ints.T)


def solution(mesh):
    in_specs = (
        P("section", "expert"),
        P(),
        P("expert", None, "section"),
        P("expert", None, "section"),
        P("expert", "section", None),
        P(),
        P(),
    )
    run = functools.partial(
        body, sections=mesh.shape["section"], experts=mesh.shape["expert"]
    )
    return jax.shard_map(
        run, mesh=mesh, in_specs=in_specs, out_specs=P("section", "expert"), check_vma=False
    )
```

time: 207 us -> 38.3 us (0.19)
  blocking collectives: 77.5 us -> 0 us
  waiting for transfers between devices: 77.3 us -> 0 us
  Pallas kernels: 0 us -> 36.7 us
  local copies, waits for them, and re-layouts: 16.4 us -> 1.42 us
  between operations: 14.1 us -> 0.01 us
  matrix products: 10.1 us -> 0 us
  starting transfers between devices: 6.54 us -> 0 us
  other arithmetic: 4.59 us -> 0 us
    unnamed x1 -> x0, blocking collectives: 70.4 us -> none
    all_gather x1 -> x0, waiting for transfers between devices: 45.7 us -> none  [body(): routed = lax.all_gather(picked, 'section', axis=0, tiled=True)]
    pallas_call x0 -> x1, Pallas kernels: none -> 36.7 us  [body(): pl.pallas_call(functools.partial(kernel, depth), out_shape=jax.ShapeDtype...]
    reduce_scatter x1 -> x0, waiting for transfers between devices: 25.3 us -> none  [body(): lax.psum_scatter(token_term, 'expert', scatter_dimension=1, tiled=True)]
    unnamed x11 -> x1, local copies, waits for them, and re-layouts: 14.8 us -> 1.42 us
    dot_general x3 -> x0, matrix products: 10.1 us -> none  [the longest x1 5.53 us: expert_product(): return jnp.dot(hidden_act, down_w, preferred_element_type=jnp.float32)]
    all_gather x1 -> x0, blocking collectives: 7.08 us -> none  [body(): full_rows = lax.all_gather(tokens, 'expert', axis=1, tiled=True)]
    unnamed x2 -> x0, starting transfers between devices: 6.5 us -> none
  transfers between devices with their start and end apart: 4 -> 0, of which waited for: 3 -> 0; matrix products, arithmetic and copies ran while one was open for 1% -> 0% of each run, Pallas kernels for 0% -> 0%
where the time goes in v1:
time: 38.3 us; the launch traced here: 38.1 us
  Pallas kernels  36.7 us (96%)
  local copies, waits for them, and re-layouts  1.42 us (4%)
    pallas_call x1, Pallas kernels, body(): pl.pallas_call(functools.partial(kernel, depth), out_shape=jax.ShapeDtype...  36.7 us
    unnamed x1, local copies, waits for them, and re-layouts  1.42 us

profile of v1, /device:TPU:0, one launch (start us, length us, event | category | flops | bytes accessed | tf_op | source)
XLA Modules:
  0.0 38.1 jit_solution(16209850278831679731)
XLA Ops:
  0.0 36.7 %shard_map.73 = bf16[16,1536]{1,0:T(8,128)(2,1)} custom-call(bf16[16,1536]{1,0:T(8,128)(2,1)} %tok.1, f32[1,6144]{1,0:T(1,128)} %bitcast.3, bf16[1,6144,256]{2,1,0:T(8,128)(2,1)} %wg.1, bf16[1,6144,256]{2,1,0:T(8,128)(2,1)} %wu.1, bf16[1,256,6144]{2,1,0:T(8,128)(2,1)} %wd.1, s32[2,128]{1,0:T(2,128)} %bitcast.4, s32[2,128]{1,0:T(2,128)} %bitcast.5), custom_call_target="tpu_custom_call" | custom-call | tf_op jit(solution)/shard_map/pallas_call | solution.py:254
  36.7 1.4 %copy.9 = bf16[16,1536]{1,0:T(8,128)(2,1)} copy(bf16[16,1536]{1,0:T(8,128)(2,1)} %shard_map.73) | data formatting | bytes 98304

commit v2 on v1

--- a/solution.py
+++ b/solution.py
@@ -12,6 +12,7 @@
 BF16 = jnp.bfloat16
 F32 = jnp.float32
 TILE = 128
+LANES = 128
 
 
 def flip(index, mask):
@@ -25,7 +26,7 @@
 
 def kernel(
     depth, tok, gains, wg, wu, wd, ids, ints, out,
-    x, xn, w_in, w_out, gains_v, ids_v, ints_v, inner, weight,
+    x, xn, w_in, w_out, gains_v, ids_v, ints_v, inner, weight, ss, acc,
     own, sib_s, sib_r, b_s, b_r, a_s, a_r, z_s, z_r,
     load_sem, in_recv, in_sib_recv, in_z_send, in_a_send, in_b_send, in_sib_send,
     sib_send, sib_recv, b_send, b_recv, a_send, a_recv, z_send, z_recv,
@@ -57,27 +58,28 @@
     sib_dev = (section, py * 2 + 1 - core)
     z_devs = [(flip(z, k) * 2 + px, expert) for k in range(1, depth)]
 
+    own_block = x.at[expert, rows_of(section)]
+    tok_load = pltpu.make_async_copy(tok, own_block, load_sem.at[0])
+    tok_load.start()
     loads = [
-        pltpu.make_async_copy(tok, x.at[expert, rows_of(section)], load_sem.at[0]),
-        pltpu.make_async_copy(wg.at[0], w_in.at[:, pl.ds(0, hid)], load_sem.at[1]),
-        pltpu.make_async_copy(wu.at[0], w_in.at[:, pl.ds(hid, hid)], load_sem.at[2]),
         pltpu.make_async_copy(gains, gains_v, load_sem.at[3]),
         pltpu.make_async_copy(ids, ids_v, load_sem.at[4]),
         pltpu.make_async_copy(ints, ints_v, load_sem.at[5]),
+        pltpu.make_async_copy(wg.at[0], w_in.at[:, pl.ds(0, hid)], load_sem.at[1]),
+        pltpu.make_async_copy(wu.at[0], w_in.at[:, pl.ds(hid, hid)], load_sem.at[2]),
     ] + [
         pltpu.make_async_copy(
             wd.at[0, :, pl.ds(e * width, width)], w_out.at[e], load_sem.at[6 + e]
         )
         for e in range(x.shape[0])
     ]
-    for load in loads:
-        load.start()
 
     barrier = pltpu.get_barrier_semaphore()
     partners = z_devs + [a_dev, b_dev, sib_dev]
     for partner in partners:
         pl.semaphore_signal(barrier, inc=1, device_id=partner, device_id_type=MESH)
     pl.semaphore_wait(barrier, len(partners))
+    tok_load.wait()
 
     pending = []
 
@@ -114,10 +116,12 @@
         return here
 
     for k in range(1, depth):
-        push(tok, z, i, j, in_z_send.at[k - 1], z_devs[k - 1])
-    push(tok, z, i, j, in_a_send.at[0], a_dev)
-    push(tok, z, i, j, in_b_send.at[0], b_dev)
-    push_sib(tok, z, i, j)
+        push(own_block, z, i, j, in_z_send.at[k - 1], z_devs[k - 1])
+    push(own_block, z, i, j, in_a_send.at[0], a_dev)
+    push(own_block, z, i, j, in_b_send.at[0], b_dev)
+    push_sib(own_block, z, i, j)
+    for load in loads:
+        load.start()
     for k in range(1, depth):
         zz = flip(z, k)
         here = arrived(zz, i, j)
@@ -129,27 +133,6 @@
         here = arrived(zz, i, 1 - j)
         push(here, zz, i, 1 - j, in_b_send.at[depth + k], b_dev)
         push_sib(here, zz, i, 1 - j)
-    for jj in (j, 1 - j):
-        for k in range(depth):
-            zz = flip(z, k)
-            push_sib(arrived(zz, 1 - i, jj), zz, 1 - i, jj)
-
-    for load in loads:
-        load.wait()
-    chosen = jnp.where(ids_v[...] == expert, ints_v[...].astype(F32) / 65536.0, 0.0)
-    row = jnp.sum(chosen, axis=0, keepdims=True)
-    weight[...] = jnp.broadcast_to(row, (8, total)).T[:, :1]
-
-    for sec in range(2 * depth):
-        for yy in range(2):
-            here = x.at[yy * 2 + 1 - core, rows_of(sec)]
-            pltpu.make_async_remote_copy(
-                src_ref=here, dst_ref=here, send_sem=in_z_send.at[0],
-                recv_sem=in_sib_recv.at[sec * 2 + yy],
-                device_id=sib_dev, device_id_type=MESH,
-            ).wait_recv()
-
-    slices = range(x.shape[0])
 
     def tiles(body):
         if total == TILE:
@@ -159,21 +142,59 @@
             def _(t):
                 body(pl.ds(pl.multiple_of(t * TILE, TILE), TILE))
 
-    def hidden(span):
-        squares = 0.0
-        for e in slices:
-            part = x[e, span].astype(F32)
-            squares = squares + jnp.sum(part * part, axis=-1, keepdims=True)
-        scale = lax.rsqrt(squares / features + EPS)
-        both = jnp.zeros((TILE, 2 * hid), F32)
-        for e in slices:
-            cols = pl.ds(e * width, width)
-            xn[e] = (x[e, span].astype(F32) * scale * gains_v[:, cols]).astype(BF16)
-            both = both + jnp.dot(xn[e], w_in[cols], preferred_element_type=F32)
+    def project(e, first):
+        def one(span):
+            squares = jnp.zeros((TILE, LANES), F32) if first else ss[span]
+            for c in range(0, width, LANES):
+                cols = pl.ds(c, LANES)
+                part = x[e, span, cols].astype(F32)
+                squares = squares + part * part
+                xn[:, cols] = (part * gains_v[e, :, cols]).astype(BF16)
+            ss[span] = squares
+            product = jnp.dot(
+                xn[...], w_in[pl.ds(pl.multiple_of(e * width, width), width)],
+                preferred_element_type=F32,
+            )
+            acc[span] = product if first else acc[span] + product
+        tiles(one)
+
+    def forward(jj, ks):
+        for k in ks:
+            zz = flip(z, k)
+            push_sib(arrived(zz, 1 - i, jj), zz, 1 - i, jj)
+
+    def sib_slice(yy):
+        for sec in range(2 * depth):
+            here = x.at[yy * 2 + 1 - core, rows_of(sec)]
+            pltpu.make_async_remote_copy(
+                src_ref=here, dst_ref=here, send_sem=in_z_send.at[0],
+                recv_sem=in_sib_recv.at[sec * 2 + yy],
+                device_id=sib_dev, device_id_type=MESH,
+            ).wait_recv()
+
+    for load in loads:
+        load.wait()
+    chosen = jnp.where(ids_v[...] == expert, ints_v[...].astype(F32) / 65536.0, 0.0)
+    row = jnp.sum(chosen, axis=0, keepdims=True)
+    weight[...] = jnp.broadcast_to(row, (8, total)).T[:, :1]
+
+    forward(j, range(depth))
+    project(py * 2 + core, True)
+    forward(1 - j, range(depth // 2))
+    sib_slice(py)
+    project(py * 2 + 1 - core, False)
+    forward(1 - j, range(depth // 2, depth))
+    project((1 - py) * 2 + core, False)
+    sib_slice(1 - py)
+    project((1 - py) * 2 + 1 - core, False)
+
+    def activate(span):
+        mean_sq = jnp.sum(ss[span], axis=-1, keepdims=True) / features
+        both = acc[span] * lax.rsqrt(mean_sq + EPS)
         gate, up = both[:, :hid], both[:, hid:]
         inner[span] = (gate / (1.0 + jnp.exp(-gate)) * up).astype(BF16)
 
-    tiles(hidden)
+    tiles(activate)
 
     def down(e, target, kind):
         def one(span):
@@ -182,21 +203,19 @@
             ).astype(kind)
         tiles(one)
 
-    for n, yy in enumerate((1 - py, py)):
-        down(yy * 2 + 1 - core, sib_s.at[yy], BF16)
-        copy = pltpu.make_async_remote_copy(
+    def sib_copy(yy):
+        return pltpu.make_async_remote_copy(
             src_ref=sib_s.at[yy], dst_ref=sib_r.at[yy], send_sem=sib_send.at[yy],
             recv_sem=sib_recv.at[yy], device_id=sib_dev, device_id_type=MESH,
         )
+
+    def partials(yy):
+        down(yy * 2 + 1 - core, sib_s.at[yy], BF16)
+        copy = sib_copy(yy)
         copy.start()
         pending.append(copy)
-    for yy in (1 - py, py):
         down(yy * 2 + core, own.at[yy], F32)
-    for yy in (1 - py, py):
-        pltpu.make_async_remote_copy(
-            src_ref=sib_s.at[yy], dst_ref=sib_r.at[yy], send_sem=sib_send.at[yy],
-            recv_sem=sib_recv.at[yy], device_id=sib_dev, device_id_type=MESH,
-        ).wait_recv()
+        copy.wait_recv()
 
     def pair(zz, ii, jj):
         sec, yy = place(zz, ii, jj)
@@ -221,7 +240,8 @@
         return target[slot].astype(F32)
 
     order = list(range(1, depth)) + [0]
-    for jj in (1 - j, j):
+    for yy, jj in ((1 - py, 1 - j), (py, j)):
+        partials(yy)
         for k in order:
             zz = flip(z, k)
             slot = jj * depth + zz
@@ -258,14 +278,16 @@
         out_specs=pl.BlockSpec(memory_space=pltpu.VMEM),
         scratch_shapes=[
             pltpu.VMEM((experts, total, width), BF16),
-            pltpu.VMEM((experts, TILE, width), BF16),
+            pltpu.VMEM((TILE, width), BF16),
             pltpu.VMEM((features, 2 * hid), BF16),
             pltpu.VMEM((experts, hid, width), BF16),
-            pltpu.VMEM((1, features), F32),
+            pltpu.VMEM((experts, 1, width), F32),
             pltpu.VMEM((top, total), jnp.int32),
             pltpu.VMEM((top, total), jnp.int32),
             pltpu.VMEM((total, hid), BF16),
             pltpu.VMEM((total, 1), F32),
+            pltpu.VMEM((total, LANES), F32),
+            pltpu.VMEM((total, 2 * hid), F32),
             pltpu.VMEM((2, total, width), F32),
             pltpu.VMEM((2, total, width), BF16),
             pltpu.VMEM((2, total, width), BF16),
@@ -286,7 +308,7 @@
         compiler_params=pltpu.CompilerParams(
             collective_id=0, has_side_effects=True, vmem_limit_bytes=62 * 1024 * 1024,
         ),
-    )(tokens, gains.reshape(1, features), w_gate, w_up, w_down, expert_ids.T, gate_ints.T)
+    )(tokens, gains.reshape(experts, 1, width), w_gate, w_up, w_down, expert_ids.T, gate_ints.T)
 
 
 def solution(mesh):

time: 38.3 us -> 36.6 us (0.956)
  Pallas kernels: 36.7 us -> 35 us
    pallas_call x1, Pallas kernels: 36.7 us -> 35 us  [body(): pl.pallas_call(functools.partial(kernel, depth), out_shape=jax.ShapeDtype...]
where the time goes in v2:
time: 36.6 us; the launch traced here: 36.4 us
  Pallas kernels  35 us (96%)
  local copies, waits for them, and re-layouts  1.42 us (4%)
    pallas_call x1, Pallas kernels, body(): pl.pallas_call(functools.partial(kernel, depth), out_shape=jax.ShapeDtype...  35 us
    unnamed x1, local copies, waits for them, and re-layouts  1.42 us

profile of v2, /device:TPU:0, one launch (start us, length us, event | category | flops | bytes accessed | tf_op | source)
XLA Modules:
  0.0 36.4 jit_solution(2383071205327395821)
XLA Ops:
  0.0 35.0 %shard_map.73 = bf16[16,1536]{1,0:T(8,128)(2,1)} custom-call(bf16[16,1536]{1,0:T(8,128)(2,1)} %tok.1, f32[4,1,1536]{2,1,0:T(1,128)} %bitcast.3, bf16[1,6144,256]{2,1,0:T(8,128)(2,1)} %wg.1, bf16[1,6144,256]{2,1,0:T(8,128)(2,1)} %wu.1, bf16[1,256,6144]{2,1,0:T(8,128)(2,1)} %wd.1, s32[2,128]{1,0:T(2,128)} %bitcast.4, s32[2,128]{1,0:T(2,128)} %bitcast.5), custom_call_target="tpu_custom_call" | custom-call | tf_op jit(solution)/shard_map/pallas_call | solution.py:274
  35.0 1.4 %copy.9 = bf16[16,1536]{1,0:T(8,128)(2,1)} copy(bf16[16,1536]{1,0:T(8,128)(2,1)} %shard_map.73) | data formatting | bytes 98304

commit v3 on v2

--- a/solution.py
+++ b/solution.py
@@ -27,9 +27,9 @@
 def kernel(
     depth, tok, gains, wg, wu, wd, ids, ints, out,
     x, xn, w_in, w_out, gains_v, ids_v, ints_v, inner, weight, ss, acc,
-    own, sib_s, sib_r, b_s, b_r, a_s, a_r, z_s, z_r,
+    own, b_s, b_r, a_s, a_r, z_s, z_r,
     load_sem, in_recv, in_sib_recv, in_z_send, in_a_send, in_b_send, in_sib_send,
-    sib_send, sib_recv, b_send, b_recv, a_send, a_recv, z_send, z_recv,
+    w_send, w_recv, inner_send, inner_recv, b_send, b_recv, a_send, a_recv, z_send, z_recv,
 ):
     section, expert = lax.axis_index("section"), lax.axis_index("expert")
     z, px = lax.div(section, 2), lax.rem(section, 2)
@@ -62,22 +62,34 @@
     tok_load = pltpu.make_async_copy(tok, own_block, load_sem.at[0])
     tok_load.start()
     loads = [
-        pltpu.make_async_copy(gains, gains_v, load_sem.at[3]),
-        pltpu.make_async_copy(ids, ids_v, load_sem.at[4]),
-        pltpu.make_async_copy(ints, ints_v, load_sem.at[5]),
-        pltpu.make_async_copy(wg.at[0], w_in.at[:, pl.ds(0, hid)], load_sem.at[1]),
-        pltpu.make_async_copy(wu.at[0], w_in.at[:, pl.ds(hid, hid)], load_sem.at[2]),
-    ] + [
+        pltpu.make_async_copy(gains, gains_v, load_sem.at[1]),
+        pltpu.make_async_copy(ids, ids_v, load_sem.at[2]),
+        pltpu.make_async_copy(ints, ints_v, load_sem.at[3]),
+    ]
+    for e in range(x.shape[0]):
+        part = pl.ds(e * width, width)
+        for n, w in enumerate((wg, wu)):
+            loads.append(
+                pltpu.make_async_copy(
+                    w.at[0, part], w_in.at[part, pl.ds(n * hid, hid)], load_sem.at[4 + 2 * e + n]
+                )
+            )
+
+    def wd_slice(e):
+        return wd.at[0, :, pl.ds(pl.multiple_of(e * width, width), width)]
+
+    out_loads = [
         pltpu.make_async_copy(
-            wd.at[0, :, pl.ds(e * width, width)], w_out.at[e], load_sem.at[6 + e]
-        )
-        for e in range(x.shape[0])
+            wd_slice(yy * 2 + core), w_out.at[0, yy], load_sem.at[4 + 2 * x.shape[0] + yy]
+        )
+        for yy in range(2)
     ]
-
     barrier = pltpu.get_barrier_semaphore()
     partners = z_devs + [a_dev, b_dev, sib_dev]
     for partner in partners:
         pl.semaphore_signal(barrier, inc=1, device_id=partner, device_id_type=MESH)
+    for load in loads + out_loads:
+        load.start()
     pl.semaphore_wait(barrier, len(partners))
     tok_load.wait()
 
@@ -120,8 +132,17 @@
     push(own_block, z, i, j, in_a_send.at[0], a_dev)
     push(own_block, z, i, j, in_b_send.at[0], b_dev)
     push_sib(own_block, z, i, j)
-    for load in loads:
-        load.start()
+    w_copies = [
+        pltpu.make_async_remote_copy(
+            src_ref=wd_slice(yy * 2 + 1 - core), dst_ref=w_out.at[1, yy],
+            send_sem=w_send.at[yy], recv_sem=w_recv.at[yy],
+            device_id=sib_dev, device_id_type=MESH,
+        )
+        for yy in range(2)
+    ]
+    for copy in w_copies:
+        copy.start()
+        pending.append(copy)
     for k in range(1, depth):
         zz = flip(z, k)
         here = arrived(zz, i, j)
@@ -172,13 +193,13 @@
                 device_id=sib_dev, device_id_type=MESH,
             ).wait_recv()
 
+    forward(j, range(depth))
     for load in loads:
         load.wait()
-    chosen = jnp.where(ids_v[...] == expert, ints_v[...].astype(F32) / 65536.0, 0.0)
-    row = jnp.sum(chosen, axis=0, keepdims=True)
-    weight[...] = jnp.broadcast_to(row, (8, total)).T[:, :1]
-
-    forward(j, range(depth))
+    for n, which in enumerate((expert, py * 2 + 1 - core)):
+        chosen = jnp.where(ids_v[...] == which, ints_v[...].astype(F32) / 65536.0, 0.0)
+        row = jnp.sum(chosen, axis=0, keepdims=True)
+        weight[n] = jnp.broadcast_to(row, (8, total)).T[:, :1]
     project(py * 2 + core, True)
     forward(1 - j, range(depth // 2))
     sib_slice(py)
@@ -192,35 +213,37 @@
         mean_sq = jnp.sum(ss[span], axis=-1, keepdims=True) / features
         both = acc[span] * lax.rsqrt(mean_sq + EPS)
         gate, up = both[:, :hid], both[:, hid:]
-        inner[span] = (gate / (1.0 + jnp.exp(-gate)) * up).astype(BF16)
+        inner[0, span] = (gate / (1.0 + jnp.exp(-gate)) * up).astype(BF16)
 
     tiles(activate)
 
-    def down(e, target, kind):
+    inner_copy = pltpu.make_async_remote_copy(
+        src_ref=inner.at[0], dst_ref=inner.at[1], send_sem=inner_send, recv_sem=inner_recv,
+        device_id=sib_dev, device_id_type=MESH,
+    )
+    inner_copy.start()
+    pending.append(inner_copy)
+
+    def down(yy, n):
         def one(span):
-            target[span] = (
-                jnp.dot(inner[span], w_out[e], preferred_element_type=F32) * weight[span]
-            ).astype(kind)
+            product = (
+                jnp.dot(inner[n, span], w_out[n, yy], preferred_element_type=F32) * weight[n, span]
+            )
+            own[yy, span] = own[yy, span] + product if n else product
         tiles(one)
 
-    def sib_copy(yy):
-        return pltpu.make_async_remote_copy(
-            src_ref=sib_s.at[yy], dst_ref=sib_r.at[yy], send_sem=sib_send.at[yy],
-            recv_sem=sib_recv.at[yy], device_id=sib_dev, device_id_type=MESH,
-        )
-
-    def partials(yy):
-        down(yy * 2 + 1 - core, sib_s.at[yy], BF16)
-        copy = sib_copy(yy)
-        copy.start()
-        pending.append(copy)
-        down(yy * 2 + core, own.at[yy], F32)
+    for load in out_loads:
+        load.wait()
+    for yy in (1 - py, py):
+        down(yy, 0)
+    for copy in w_copies:
         copy.wait_recv()
-
-    def pair(zz, ii, jj):
+    inner_copy.wait_recv()
+
+    def mine(zz, ii, jj):
         sec, yy = place(zz, ii, jj)
         span = rows_of(sec)
-        return own[yy, span] + sib_r[yy, span].astype(F32)
+        return own[yy, span]
 
     def send(value, source, source_slot, target, target_slot, send_sem, recv_sem, dev):
         source[source_slot] = value.astype(BF16)
@@ -241,18 +264,18 @@
 
     order = list(range(1, depth)) + [0]
     for yy, jj in ((1 - py, 1 - j), (py, j)):
-        partials(yy)
+        down(yy, 1)
         for k in order:
             zz = flip(z, k)
             slot = jj * depth + zz
-            send(pair(zz, 1 - i, jj), b_s, slot, b_r, slot, b_send, b_recv, b_dev)
+            send(mine(zz, 1 - i, jj), b_s, slot, b_r, slot, b_send, b_recv, b_dev)
     for k in order:
         zz = flip(z, k)
-        value = pair(zz, i, 1 - j) + take(b_r, (1 - j) * depth + zz, b_recv)
+        value = mine(zz, i, 1 - j) + take(b_r, (1 - j) * depth + zz, b_recv)
         send(value, a_s, zz, a_r, zz, a_send, a_recv, a_dev)
     for k in order:
         zz = flip(z, k)
-        value = pair(zz, i, j) + take(b_r, j * depth + zz, b_recv) + take(a_r, zz, a_recv)
+        value = mine(zz, i, j) + take(b_r, j * depth + zz, b_recv) + take(a_r, zz, a_recv)
         if k:
             send(value, z_s, zz, z_r, z, z_send, z_recv, z_devs[k - 1])
     for k in range(1, depth):
@@ -280,27 +303,25 @@
             pltpu.VMEM((experts, total, width), BF16),
             pltpu.VMEM((TILE, width), BF16),
             pltpu.VMEM((features, 2 * hid), BF16),
-            pltpu.VMEM((experts, hid, width), BF16),
+            pltpu.VMEM((2, 2, hid, width), BF16),
             pltpu.VMEM((experts, 1, width), F32),
             pltpu.VMEM((top, total), jnp.int32),
             pltpu.VMEM((top, total), jnp.int32),
-            pltpu.VMEM((total, hid), BF16),
-            pltpu.VMEM((total, 1), F32),
+            pltpu.VMEM((2, total, hid), BF16),
+            pltpu.VMEM((2, total, 1), F32),
             pltpu.VMEM((total, LANES), F32),
             pltpu.VMEM((total, 2 * hid), F32),
             pltpu.VMEM((2, total, width), F32),
-            pltpu.VMEM((2, total, width), BF16),
-            pltpu.VMEM((2, total, width), BF16),
             pltpu.VMEM((2 * depth, rows, width), BF16),
             pltpu.VMEM((2 * depth, rows, width), BF16),
             pltpu.VMEM((depth, rows, width), BF16),
             pltpu.VMEM((depth, rows, width), BF16),
             pltpu.VMEM((depth, rows, width), BF16),
             pltpu.VMEM((depth, rows, width), BF16),
-            dma((6 + experts,)),
+            dma((6 + 2 * experts,)),
             dma((blocks,)), dma((blocks,)),
             dma((depth,)), dma((depth,)), dma((2 * depth,)), dma((blocks,)),
-            dma((2,)), dma((2,)),
+            dma((2,)), dma((2,)), dma, dma,
             dma((2 * depth,)), dma((2 * depth,)),
             dma((depth,)), dma((depth,)),
             dma((depth,)), dma((depth,)),

time: 36.6 us -> 36.3 us (level)
  no operation moved by 1% of the time
where the time goes in v3:
time: 36.3 us; the launch traced here: 36.1 us
  Pallas kernels  34.7 us (96%)
  local copies, waits for them, and re-layouts  1.42 us (4%)
    pallas_call x1, Pallas kernels, body(): pl.pallas_call(functools.partial(kernel, depth), out_shape=jax.ShapeDtype...  34.7 us
    unnamed x1, local copies, waits for them, and re-layouts  1.42 us

profile of v3, /device:TPU:0, one launch (start us, length us, event | category | flops | bytes accessed | tf_op | source)
XLA Modules:
  0.0 36.1 jit_solution(17276861891606398246)
XLA Ops:
  0.0 34.7 %shard_map.73 = bf16[16,1536]{1,0:T(8,128)(2,1)} custom-call(bf16[16,1536]{1,0:T(8,128)(2,1)} %tok.1, f32[4,1,1536]{2,1,0:T(1,128)} %bitcast.3, bf16[1,6144,256]{2,1,0:T(8,128)(2,1)} %wg.1, bf16[1,6144,256]{2,1,0:T(8,128)(2,1)} %wu.1, bf16[1,256,6144]{2,1,0:T(8,128)(2,1)} %wd.1, s32[2,128]{1,0:T(2,128)} %bitcast.4, s32[2,128]{1,0:T(2,128)} %bitcast.5), custom_call_target="tpu_custom_call" | custom-call | tf_op jit(solution)/shard_map/pallas_call | solution.py:297
  34.7 1.4 %copy.9 = bf16[16,1536]{1,0:T(8,128)(2,1)} copy(bf16[16,1536]{1,0:T(8,128)(2,1)} %shard_map.73) | data formatting | bytes 98304

commit v4 on v3

--- a/solution.py
+++ b/solution.py
@@ -44,21 +44,21 @@
     def place(zz, ii, jj):
         yy = ii * (1 - core) + jj * core
         xx = jj * (1 - core) + ii * core
-        return zz * 2 + xx, yy
-
-    def rows_of(sec):
-        return pl.ds(pl.multiple_of(sec * rows, rows), rows)
+        return xx, yy
+
+    def spot(zz, xx, count=1):
+        return pl.ds(pl.multiple_of((xx * depth + zz) * rows, rows), count * rows)
 
     def device(zz, ii, jj):
-        sec, yy = place(zz, ii, jj)
-        return sec, yy * 2 + core
+        xx, yy = place(zz, ii, jj)
+        return zz * 2 + xx, yy * 2 + core
 
     a_dev = device(z, i, 1 - j)
     b_dev = device(z, 1 - i, j)
     sib_dev = (section, py * 2 + 1 - core)
     z_devs = [(flip(z, k) * 2 + px, expert) for k in range(1, depth)]
 
-    own_block = x.at[expert, rows_of(section)]
+    own_block = x.at[expert, spot(z, px)]
     tok_load = pltpu.make_async_copy(tok, own_block, load_sem.at[0])
     tok_load.start()
     loads = [
@@ -93,45 +93,46 @@
     pl.semaphore_wait(barrier, len(partners))
     tok_load.wait()
 
-    pending = []
-
     def block(zz, ii, jj):
-        sec, yy = place(zz, ii, jj)
-        return x.at[yy * 2 + core, rows_of(sec)]
+        xx, yy = place(zz, ii, jj)
+        return x.at[yy * 2 + core, spot(zz, xx)]
 
     def push(source, zz, ii, jj, send_sem, target):
-        copy = pltpu.make_async_remote_copy(
+        pltpu.make_async_remote_copy(
             src_ref=source, dst_ref=block(zz, ii, jj), send_sem=send_sem,
             recv_sem=in_recv.at[(zz * 2 + ii) * 2 + jj],
             device_id=target, device_id_type=MESH,
-        )
-        copy.start()
-        pending.append(copy)
-
-    def push_sib(source, zz, ii, jj):
-        sec, yy = place(zz, ii, jj)
-        copy = pltpu.make_async_remote_copy(
-            src_ref=source, dst_ref=block(zz, ii, jj), send_sem=in_sib_send.at[sec * 2 + yy],
-            recv_sem=in_sib_recv.at[sec * 2 + yy],
+        ).start()
+
+    def push_sib(ii, jj, first, count):
+        xx, yy = place(z, ii, jj)
+        here = x.at[yy * 2 + core, spot(first, xx, count)]
+        pltpu.make_async_remote_copy(
+            src_ref=here, dst_ref=here, send_sem=in_sib_send, recv_sem=in_sib_recv.at[yy],
             device_id=sib_dev, device_id_type=MESH,
-        )
-        copy.start()
-        pending.append(copy)
+        ).start()
+
+    def wait_recv(ref, sem):
+        pltpu.make_async_remote_copy(
+            src_ref=ref, dst_ref=ref, send_sem=in_z_send, recv_sem=sem,
+            device_id=sib_dev, device_id_type=MESH,
+        ).wait_recv()
+
+    def wait_send(ref, sem):
+        pltpu.make_async_remote_copy(
+            src_ref=ref, dst_ref=ref, send_sem=sem, recv_sem=in_recv.at[0],
+            device_id=sib_dev, device_id_type=MESH,
+        ).wait_send()
 
     def arrived(zz, ii, jj):
         here = block(zz, ii, jj)
-        pltpu.make_async_remote_copy(
-            src_ref=here, dst_ref=here, send_sem=in_z_send.at[0],
-            recv_sem=in_recv.at[(zz * 2 + ii) * 2 + jj],
-            device_id=sib_dev, device_id_type=MESH,
-        ).wait_recv()
+        wait_recv(here, in_recv.at[(zz * 2 + ii) * 2 + jj])
         return here
 
     for k in range(1, depth):
-        push(own_block, z, i, j, in_z_send.at[k - 1], z_devs[k - 1])
-    push(own_block, z, i, j, in_a_send.at[0], a_dev)
-    push(own_block, z, i, j, in_b_send.at[0], b_dev)
-    push_sib(own_block, z, i, j)
+        push(own_block, z, i, j, in_z_send, z_devs[k - 1])
+    push(own_block, z, i, j, in_a_send, a_dev)
+    push(own_block, z, i, j, in_b_send, b_dev)
     w_copies = [
         pltpu.make_async_remote_copy(
             src_ref=wd_slice(yy * 2 + 1 - core), dst_ref=w_out.at[1, yy],
@@ -142,18 +143,16 @@
     ]
     for copy in w_copies:
         copy.start()
-        pending.append(copy)
     for k in range(1, depth):
         zz = flip(z, k)
         here = arrived(zz, i, j)
-        push(here, zz, i, j, in_a_send.at[k], a_dev)
-        push(here, zz, i, j, in_b_send.at[k], b_dev)
-        push_sib(here, zz, i, j)
+        push(here, zz, i, j, in_a_send, a_dev)
+        push(here, zz, i, j, in_b_send, b_dev)
+    push_sib(i, j, 0, depth)
     for k in range(depth):
         zz = flip(z, k)
-        here = arrived(zz, i, 1 - j)
-        push(here, zz, i, 1 - j, in_b_send.at[depth + k], b_dev)
-        push_sib(here, zz, i, 1 - j)
+        push(arrived(zz, i, 1 - j), zz, i, 1 - j, in_b_send, b_dev)
+    push_sib(i, 1 - j, 0, depth)
 
     def tiles(body):
         if total == TILE:
@@ -179,32 +178,30 @@
             acc[span] = product if first else acc[span] + product
         tiles(one)
 
-    def forward(jj, ks):
+    half = depth // 2
+
+    def forward(jj, ks, first):
         for k in ks:
-            zz = flip(z, k)
-            push_sib(arrived(zz, 1 - i, jj), zz, 1 - i, jj)
+            arrived(flip(z, k), 1 - i, jj)
+        push_sib(1 - i, jj, first, len(ks))
 
     def sib_slice(yy):
-        for sec in range(2 * depth):
-            here = x.at[yy * 2 + 1 - core, rows_of(sec)]
-            pltpu.make_async_remote_copy(
-                src_ref=here, dst_ref=here, send_sem=in_z_send.at[0],
-                recv_sem=in_sib_recv.at[sec * 2 + yy],
-                device_id=sib_dev, device_id_type=MESH,
-            ).wait_recv()
-
-    forward(j, range(depth))
+        wait_recv(x.at[yy * 2 + 1 - core], in_sib_recv.at[yy])
+
+    forward(j, range(depth), 0)
     for load in loads:
         load.wait()
     for n, which in enumerate((expert, py * 2 + 1 - core)):
         chosen = jnp.where(ids_v[...] == which, ints_v[...].astype(F32) / 65536.0, 0.0)
         row = jnp.sum(chosen, axis=0, keepdims=True)
-        weight[n] = jnp.broadcast_to(row, (8, total)).T[:, :1]
+        column = jnp.broadcast_to(row, (8, total)).T[:, :1]
+        for sec in range(2 * depth):
+            weight[n, spot(sec // 2, sec % 2)] = column[sec * rows : (sec + 1) * rows]
     project(py * 2 + core, True)
-    forward(1 - j, range(depth // 2))
+    forward(1 - j, range(half), lax.div(z, half) * half)
     sib_slice(py)
     project(py * 2 + 1 - core, False)
-    forward(1 - j, range(depth // 2, depth))
+    forward(1 - j, range(half, depth), half - lax.div(z, half) * half)
     project((1 - py) * 2 + core, False)
     sib_slice(1 - py)
     project((1 - py) * 2 + 1 - core, False)
@@ -222,7 +219,6 @@
         device_id=sib_dev, device_id_type=MESH,
     )
     inner_copy.start()
-    pending.append(inner_copy)
 
     def down(yy, n):
         def one(span):
@@ -241,25 +237,18 @@
     inner_copy.wait_recv()
 
     def mine(zz, ii, jj):
-        sec, yy = place(zz, ii, jj)
-        span = rows_of(sec)
-        return own[yy, span]
-
-    def send(value, source, source_slot, target, target_slot, send_sem, recv_sem, dev):
-        source[source_slot] = value.astype(BF16)
-        copy = pltpu.make_async_remote_copy(
-            src_ref=source.at[source_slot], dst_ref=target.at[target_slot],
-            send_sem=send_sem.at[source_slot], recv_sem=recv_sem.at[target_slot],
-            device_id=dev, device_id_type=MESH,
-        )
-        copy.start()
-        pending.append(copy)
+        xx, yy = place(zz, ii, jj)
+        return own[yy, spot(zz, xx)]
+
+    def send(value, source, target, slot, send_sem, recv_sem, dev):
+        source[slot] = value.astype(BF16)
+        pltpu.make_async_remote_copy(
+            src_ref=source.at[slot], dst_ref=target.at[slot], send_sem=send_sem,
+            recv_sem=recv_sem, device_id=dev, device_id_type=MESH,
+        ).start()
 
     def take(target, slot, recv_sem):
-        pltpu.make_async_remote_copy(
-            src_ref=target.at[slot], dst_ref=target.at[slot], send_sem=in_z_send.at[0],
-            recv_sem=recv_sem.at[slot], device_id=sib_dev, device_id_type=MESH,
-        ).wait_recv()
+        wait_recv(target.at[slot], recv_sem.at[slot])
         return target[slot].astype(F32)
 
     order = list(range(1, depth)) + [0]
@@ -268,21 +257,30 @@
         for k in order:
             zz = flip(z, k)
             slot = jj * depth + zz
-            send(mine(zz, 1 - i, jj), b_s, slot, b_r, slot, b_send, b_recv, b_dev)
+            send(mine(zz, 1 - i, jj), b_s, b_r, slot, b_send, b_recv.at[slot], b_dev)
+    wait_send(x.at[0, pl.ds(0, (depth - 1) * rows)], in_z_send)
+    wait_send(x.at[0, pl.ds(0, depth * rows)], in_a_send)
+    wait_send(x.at[0], in_b_send)
+    wait_send(x.at[pl.ds(0, 2)], in_sib_send)
+    for copy in w_copies + [inner_copy]:
+        copy.wait_send()
     for k in order:
         zz = flip(z, k)
         value = mine(zz, i, 1 - j) + take(b_r, (1 - j) * depth + zz, b_recv)
-        send(value, a_s, zz, a_r, zz, a_send, a_recv, a_dev)
+        send(value, a_s, a_r, zz, a_send, a_recv.at[zz], a_dev)
     for k in order:
         zz = flip(z, k)
         value = mine(zz, i, j) + take(b_r, j * depth + zz, b_recv) + take(a_r, zz, a_recv)
         if k:
-            send(value, z_s, zz, z_r, z, z_send, z_recv, z_devs[k - 1])
+            send(value, z_s, z_r, k - 1, z_send, z_recv, z_devs[k - 1])
+    value = value + x[expert, spot(z, px)].astype(F32)
+    wait_send(b_s, b_send)
+    wait_send(a_s, a_send)
+    wait_recv(z_r, z_recv)
     for k in range(1, depth):
-        value = value + take(z_r, flip(z, k), z_recv)
-    out[...] = (x[expert, rows_of(section)].astype(F32) + value).astype(BF16)
-    for copy in pending:
-        copy.wait_send()
+        value = value + z_r[k - 1].astype(F32)
+    out[...] = value.astype(BF16)
+    wait_send(z_s, z_send)
 
 
 def body(tokens, gains, w_gate, w_up, w_down, expert_ids, gate_ints, *, sections, experts):
@@ -316,15 +314,14 @@
             pltpu.VMEM((2 * depth, rows, width), BF16),
             pltpu.VMEM((depth, rows, width), BF16),
             pltpu.VMEM((depth, rows, width), BF16),
-            pltpu.VMEM((depth, rows, width), BF16),
-            pltpu.VMEM((depth, rows, width), BF16),
+            pltpu.VMEM((depth - 1, rows, width), BF16),
+            pltpu.VMEM((depth - 1, rows, width), BF16),
             dma((6 + 2 * experts,)),
-            dma((blocks,)), dma((blocks,)),
-            dma((depth,)), dma((depth,)), dma((2 * depth,)), dma((blocks,)),
+            dma((blocks,)), dma((2,)), dma, dma, dma, dma,
             dma((2,)), dma((2,)), dma, dma,
-            dma((2 * depth,)), dma((2 * depth,)),
-            dma((depth,)), dma((depth,)),
-            dma((depth,)), dma((depth,)),
+            dma, dma((2 * depth,)),
+            dma, dma((depth,)),
+            dma, dma,
         ],
         compiler_params=pltpu.CompilerParams(
             collective_id=0, has_side_effects=True, vmem_limit_bytes=62 * 1024 * 1024,

time: 36.3 us -> 35.7 us (0.983)
  Pallas kernels: 34.7 us -> 34.1 us
    pallas_call x1, Pallas kernels: 34.7 us -> 34.1 us  [body(): pl.pallas_call(functools.partial(kernel, depth), out_shape=jax.ShapeDtype...]
where the time goes in v4:
time: 35.7 us; the launch traced here: 35.6 us
  Pallas kernels  34.1 us (96%)
  local copies, waits for them, and re-layouts  1.42 us (4%)
    pallas_call x1, Pallas kernels, body(): pl.pallas_call(functools.partial(kernel, depth), out_shape=jax.ShapeDtype...  34.1 us
    unnamed x1, local copies, waits for them, and re-layouts  1.42 us

profile of v4, /device:TPU:0, one launch (start us, length us, event | category | flops | bytes accessed | tf_op | source)
XLA Modules:
  0.0 35.6 jit_solution(7564816625397962249)
XLA Ops:
  0.0 34.1 %shard_map.73 = bf16[16,1536]{1,0:T(8,128)(2,1)} custom-call(bf16[16,1536]{1,0:T(8,128)(2,1)} %tok.1, f32[4,1,1536]{2,1,0:T(1,128)} %bitcast.3, bf16[1,6144,256]{2,1,0:T(8,128)(2,1)} %wg.1, bf16[1,6144,256]{2,1,0:T(8,128)(2,1)} %wu.1, bf16[1,256,6144]{2,1,0:T(8,128)(2,1)} %wd.1, s32[2,128]{1,0:T(2,128)} %bitcast.4, s32[2,128]{1,0:T(2,128)} %bitcast.5), custom_call_target="tpu_custom_call" | custom-call | tf_op jit(solution)/shard_map/pallas_call | solution.py:295
  34.1 1.4 %copy.9 = bf16[16,1536]{1,0:T(8,128)(2,1)} copy(bf16[16,1536]{1,0:T(8,128)(2,1)} %shard_map.73) | data formatting | bytes 98304

commit v5 on v4

--- a/solution.py
+++ b/solution.py
@@ -85,12 +85,25 @@
         for yy in range(2)
     ]
     barrier = pltpu.get_barrier_semaphore()
-    partners = z_devs + [a_dev, b_dev, sib_dev]
-    for partner in partners:
+    plane = z_devs + [a_dev, b_dev]
+    for partner in plane:
         pl.semaphore_signal(barrier, inc=1, device_id=partner, device_id_type=MESH)
     for load in loads + out_loads:
         load.start()
-    pl.semaphore_wait(barrier, len(partners))
+
+    def greet_sib():
+        pl.semaphore_signal(barrier, inc=1, device_id=sib_dev, device_id_type=MESH)
+
+    @pl.when(core == 0)
+    def _():
+        pl.semaphore_wait(barrier, len(plane))
+        greet_sib()
+
+    @pl.when(core == 1)
+    def _():
+        pl.semaphore_wait(barrier, len(plane) + 1)
+        greet_sib()
+
     tok_load.wait()
 
     def block(zz, ii, jj):
@@ -141,13 +154,18 @@
         )
         for yy in range(2)
     ]
-    for copy in w_copies:
-        copy.start()
     for k in range(1, depth):
         zz = flip(z, k)
         here = arrived(zz, i, j)
         push(here, zz, i, j, in_a_send, a_dev)
         push(here, zz, i, j, in_b_send, b_dev)
+
+    @pl.when(core == 0)
+    def _():
+        pl.semaphore_wait(barrier, 1)
+
+    for copy in w_copies:
+        copy.start()
     push_sib(i, j, 0, depth)
     for k in range(depth):
         zz = flip(z, k)

time: 35.7 us -> 36.6 us (1.025)
  Pallas kernels: 34.1 us -> 35 us
    pallas_call x1, Pallas kernels: 34.1 us -> 35 us  [body(): pl.pallas_call(functools.partial(kernel, depth), out_shape=jax.ShapeDtype...]
where the time goes in v5:
time: 36.6 us; the launch traced here: 36.5 us
  Pallas kernels  35 us (96%)
  local copies, waits for them, and re-layouts  1.42 us (4%)
    pallas_call x1, Pallas kernels, body(): pl.pallas_call(functools.partial(kernel, depth), out_shape=jax.ShapeDtype...  35 us
    unnamed x1, local copies, waits for them, and re-layouts  1.42 us

profile of v5, /device:TPU:0, one launch (start us, length us, event | category | flops | bytes accessed | tf_op | source)
XLA Modules:
  0.0 36.5 jit_solution(12501177771811574845)
XLA Ops:
  0.0 35.0 %shard_map.73 = bf16[16,1536]{1,0:T(8,128)(2,1)} custom-call(bf16[16,1536]{1,0:T(8,128)(2,1)} %tok.1, f32[4,1,1536]{2,1,0:T(1,128)} %bitcast.3, bf16[1,6144,256]{2,1,0:T(8,128)(2,1)} %wg.1, bf16[1,6144,256]{2,1,0:T(8,128)(2,1)} %wu.1, bf16[1,256,6144]{2,1,0:T(8,128)(2,1)} %wd.1, s32[2,128]{1,0:T(2,128)} %bitcast.4, s32[2,128]{1,0:T(2,128)} %bitcast.5), custom_call_target="tpu_custom_call" | custom-call | tf_op jit(solution)/shard_map/pallas_call | solution.py:313
  35.1 1.4 %copy.9 = bf16[16,1536]{1,0:T(8,128)(2,1)} copy(bf16[16,1536]{1,0:T(8,128)(2,1)} %shard_map.73) | data formatting | bytes 98304

commit v6 on v4

--- a/solution.py
+++ b/solution.py
@@ -13,6 +13,7 @@
 F32 = jnp.float32
 TILE = 128
 LANES = 128
+PARTS = 2
 
 
 def flip(index, mask):
@@ -93,14 +94,20 @@
     pl.semaphore_wait(barrier, len(partners))
     tok_load.wait()
 
-    def block(zz, ii, jj):
+    def columns(p):
+        return pl.ds(p * (width // PARTS), width // PARTS)
+
+    def block(zz, ii, jj, p):
         xx, yy = place(zz, ii, jj)
-        return x.at[yy * 2 + core, spot(zz, xx)]
-
-    def push(source, zz, ii, jj, send_sem, target):
-        pltpu.make_async_remote_copy(
-            src_ref=source, dst_ref=block(zz, ii, jj), send_sem=send_sem,
-            recv_sem=in_recv.at[(zz * 2 + ii) * 2 + jj],
+        return x.at[yy * 2 + core, spot(zz, xx), columns(p)]
+
+    def mark(zz, ii, jj, p):
+        return in_recv.at[((zz * 2 + ii) * 2 + jj) * PARTS + p]
+
+    def push(zz, ii, jj, p, send_sem, target):
+        here = block(zz, ii, jj, p)
+        pltpu.make_async_remote_copy(
+            src_ref=here, dst_ref=here, send_sem=send_sem, recv_sem=mark(zz, ii, jj, p),
             device_id=target, device_id_type=MESH,
         ).start()
 
@@ -124,15 +131,14 @@
             device_id=sib_dev, device_id_type=MESH,
         ).wait_send()
 
-    def arrived(zz, ii, jj):
-        here = block(zz, ii, jj)
-        wait_recv(here, in_recv.at[(zz * 2 + ii) * 2 + jj])
-        return here
-
-    for k in range(1, depth):
-        push(own_block, z, i, j, in_z_send, z_devs[k - 1])
-    push(own_block, z, i, j, in_a_send, a_dev)
-    push(own_block, z, i, j, in_b_send, b_dev)
+    def arrived(zz, ii, jj, p):
+        wait_recv(block(zz, ii, jj, p), mark(zz, ii, jj, p))
+
+    for p in range(PARTS):
+        for k in range(1, depth):
+            push(z, i, j, p, in_z_send, z_devs[k - 1])
+        push(z, i, j, p, in_a_send, a_dev)
+        push(z, i, j, p, in_b_send, b_dev)
     w_copies = [
         pltpu.make_async_remote_copy(
             src_ref=wd_slice(yy * 2 + 1 - core), dst_ref=w_out.at[1, yy],
@@ -145,13 +151,16 @@
         copy.start()
     for k in range(1, depth):
         zz = flip(z, k)
-        here = arrived(zz, i, j)
-        push(here, zz, i, j, in_a_send, a_dev)
-        push(here, zz, i, j, in_b_send, b_dev)
+        for p in range(PARTS):
+            arrived(zz, i, j, p)
+            push(zz, i, j, p, in_a_send, a_dev)
+            push(zz, i, j, p, in_b_send, b_dev)
     push_sib(i, j, 0, depth)
     for k in range(depth):
         zz = flip(z, k)
-        push(arrived(zz, i, 1 - j), zz, i, 1 - j, in_b_send, b_dev)
+        for p in range(PARTS):
+            arrived(zz, i, 1 - j, p)
+            push(zz, i, 1 - j, p, in_b_send, b_dev)
     push_sib(i, 1 - j, 0, depth)
 
     def tiles(body):
@@ -182,7 +191,8 @@
 
     def forward(jj, ks, first):
         for k in ks:
-            arrived(flip(z, k), 1 - i, jj)
+            for p in range(PARTS):
+                arrived(flip(z, k), 1 - i, jj, p)
         push_sib(1 - i, jj, first, len(ks))
 
     def sib_slice(yy):
@@ -236,20 +246,20 @@
         copy.wait_recv()
     inner_copy.wait_recv()
 
-    def mine(zz, ii, jj):
+    def mine(zz, ii, jj, p):
         xx, yy = place(zz, ii, jj)
-        return own[yy, spot(zz, xx)]
-
-    def send(value, source, target, slot, send_sem, recv_sem, dev):
-        source[slot] = value.astype(BF16)
-        pltpu.make_async_remote_copy(
-            src_ref=source.at[slot], dst_ref=target.at[slot], send_sem=send_sem,
-            recv_sem=recv_sem, device_id=dev, device_id_type=MESH,
+        return own[yy, spot(zz, xx), columns(p)]
+
+    def send(value, source, target, slot, p, send_sem, recv_sem, dev):
+        source[slot, :, columns(p)] = value.astype(BF16)
+        pltpu.make_async_remote_copy(
+            src_ref=source.at[slot, :, columns(p)], dst_ref=target.at[slot, :, columns(p)],
+            send_sem=send_sem, recv_sem=recv_sem, device_id=dev, device_id_type=MESH,
         ).start()
 
-    def take(target, slot, recv_sem):
-        wait_recv(target.at[slot], recv_sem.at[slot])
-        return target[slot].astype(F32)
+    def take(target, slot, p, recv_sem):
+        wait_recv(target.at[slot, :, columns(p)], recv_sem.at[slot * PARTS + p])
+        return target[slot, :, columns(p)].astype(F32)
 
     order = list(range(1, depth)) + [0]
     for yy, jj in ((1 - py, 1 - j), (py, j)):
@@ -257,7 +267,11 @@
         for k in order:
             zz = flip(z, k)
             slot = jj * depth + zz
-            send(mine(zz, 1 - i, jj), b_s, b_r, slot, b_send, b_recv.at[slot], b_dev)
+            for p in range(PARTS):
+                send(
+                    mine(zz, 1 - i, jj, p), b_s, b_r, slot, p,
+                    b_send, b_recv.at[slot * PARTS + p], b_dev,
+                )
     wait_send(x.at[0, pl.ds(0, (depth - 1) * rows)], in_z_send)
     wait_send(x.at[0, pl.ds(0, depth * rows)], in_a_send)
     wait_send(x.at[0], in_b_send)
@@ -266,20 +280,31 @@
         copy.wait_send()
     for k in order:
         zz = flip(z, k)
-        value = mine(zz, i, 1 - j) + take(b_r, (1 - j) * depth + zz, b_recv)
-        send(value, a_s, a_r, zz, a_send, a_recv.at[zz], a_dev)
+        for p in range(PARTS):
+            value = mine(zz, i, 1 - j, p) + take(b_r, (1 - j) * depth + zz, p, b_recv)
+            send(value, a_s, a_r, zz, p, a_send, a_recv.at[zz * PARTS + p], a_dev)
+    last = []
     for k in order:
         zz = flip(z, k)
-        value = mine(zz, i, j) + take(b_r, j * depth + zz, b_recv) + take(a_r, zz, a_recv)
-        if k:
-            send(value, z_s, z_r, k - 1, z_send, z_recv, z_devs[k - 1])
-    value = value + x[expert, spot(z, px)].astype(F32)
+        for p in range(PARTS):
+            value = (
+                mine(zz, i, j, p)
+                + take(b_r, j * depth + zz, p, b_recv)
+                + take(a_r, zz, p, a_recv)
+            )
+            if k:
+                send(value, z_s, z_r, k - 1, p, z_send, z_recv.at[p], z_devs[k - 1])
+            else:
+                own_part = x[expert, spot(z, px), columns(p)]
+                last.append(value + own_part.astype(F32))
     wait_send(b_s, b_send)
     wait_send(a_s, a_send)
-    wait_recv(z_r, z_recv)
-    for k in range(1, depth):
-        value = value + z_r[k - 1].astype(F32)
-    out[...] = value.astype(BF16)
+    for p in range(PARTS):
+        wait_recv(z_r.at[:, :, columns(p)], z_recv.at[p])
+        value = last[p]
+        for k in range(1, depth):
+            value = value + z_r[k - 1, :, columns(p)].astype(F32)
+        out[:, columns(p)] = value.astype(BF16)
     wait_send(z_s, z_send)
 
 
@@ -317,11 +342,11 @@
             pltpu.VMEM((depth - 1, rows, width), BF16),
             pltpu.VMEM((depth - 1, rows, width), BF16),
             dma((6 + 2 * experts,)),
-            dma((blocks,)), dma((2,)), dma, dma, dma, dma,
+            dma((PARTS * blocks,)), dma((2,)), dma, dma, dma, dma,
             dma((2,)), dma((2,)), dma, dma,
-            dma, dma((2 * depth,)),
-            dma, dma((depth,)),
-            dma, dma,
+            dma, dma((PARTS * 2 * depth,)),
+            dma, dma((PARTS * depth,)),
+            dma, dma((PARTS,)),
         ],
         compiler_params=pltpu.CompilerParams(
             collective_id=0, has_side_effects=True, vmem_limit_bytes=62 * 1024 * 1024,

time: 35.7 us -> 35.4 us (level)
  no operation moved by 1% of the time
where the time goes in v6:
time: 35.4 us; the launch traced here: 35.2 us
  Pallas kernels  33.8 us (95%)
  local copies, waits for them, and re-layouts  1.42 us (4%)
    pallas_call x1, Pallas kernels, body(): pl.pallas_call(functools.partial(kernel, depth), out_shape=jax.ShapeDtype...  33.8 us
    unnamed x1, local copies, waits for them, and re-layouts  1.42 us

profile of v6, /device:TPU:0, one launch (start us, length us, event | category | flops | bytes accessed | tf_op | source)
XLA Modules:
  0.0 35.2 jit_solution(3374619558432649884)
XLA Ops:
  0.0 33.8 %shard_map.73 = bf16[16,1536]{1,0:T(8,128)(2,1)} custom-call(bf16[16,1536]{1,0:T(8,128)(2,1)} %tok.1, f32[4,1,1536]{2,1,0:T(1,128)} %bitcast.3, bf16[1,6144,256]{2,1,0:T(8,128)(2,1)} %wg.1, bf16[1,6144,256]{2,1,0:T(8,128)(2,1)} %wu.1, bf16[1,256,6144]{2,1,0:T(8,128)(2,1)} %wd.1, s32[2,128]{1,0:T(2,128)} %bitcast.4, s32[2,128]{1,0:T(2,128)} %bitcast.5), custom_call_target="tpu_custom_call" | custom-call | tf_op jit(solution)/shard_map/pallas_call | solution.py:320
  33.8 1.4 %copy.9 = bf16[16,1536]{1,0:T(8,128)(2,1)} copy(bf16[16,1536]{1,0:T(8,128)(2,1)} %shard_map.73) | data formatting | bytes 98304

commit v7 on v6

--- a/solution.py
+++ b/solution.py
@@ -147,8 +147,6 @@
         )
         for yy in range(2)
     ]
-    for copy in w_copies:
-        copy.start()
     for k in range(1, depth):
         zz = flip(z, k)
         for p in range(PARTS):
@@ -156,6 +154,8 @@
             push(zz, i, j, p, in_a_send, a_dev)
             push(zz, i, j, p, in_b_send, b_dev)
     push_sib(i, j, 0, depth)
+    for copy in w_copies:
+        copy.start()
     for k in range(depth):
         zz = flip(z, k)
         for p in range(PARTS):
@@ -261,7 +261,7 @@
         wait_recv(target.at[slot, :, columns(p)], recv_sem.at[slot * PARTS + p])
         return target[slot, :, columns(p)].astype(F32)
 
-    order = list(range(1, depth)) + [0]
+    order = list(range(half, depth)) + list(range(1, half)) + [0]
     for yy, jj in ((1 - py, 1 - j), (py, j)):
         down(yy, 1)
         for k in order:

time: 35.4 us -> 34.9 us (0.986)
  Pallas kernels: 33.8 us -> 33.3 us
    pallas_call x1, Pallas kernels: 33.8 us -> 33.3 us  [body(): pl.pallas_call(functools.partial(kernel, depth), out_shape=jax.ShapeDtype...]
where the time goes in v7:
time: 34.9 us; the launch traced here: 34.7 us
  Pallas kernels  33.3 us (95%)
  local copies, waits for them, and re-layouts  1.42 us (4%)
    pallas_call x1, Pallas kernels, body(): pl.pallas_call(functools.partial(kernel, depth), out_shape=jax.ShapeDtype...  33.3 us
    unnamed x1, local copies, waits for them, and re-layouts  1.42 us

profile of v7, /device:TPU:0, one launch (start us, length us, event | category | flops | bytes accessed | tf_op | source)
XLA Modules:
  0.0 34.7 jit_solution(1251659711803023923)
XLA Ops:
  0.0 33.3 %shard_map.73 = bf16[16,1536]{1,0:T(8,128)(2,1)} custom-call(bf16[16,1536]{1,0:T(8,128)(2,1)} %tok.1, f32[4,1,1536]{2,1,0:T(1,128)} %bitcast.3, bf16[1,6144,256]{2,1,0:T(8,128)(2,1)} %wg.1, bf16[1,6144,256]{2,1,0:T(8,128)(2,1)} %wu.1, bf16[1,256,6144]{2,1,0:T(8,128)(2,1)} %wd.1, s32[2,128]{1,0:T(2,128)} %bitcast.4, s32[2,128]{1,0:T(2,128)} %bitcast.5), custom_call_target="tpu_custom_call" | custom-call | tf_op jit(solution)/shard_map/pallas_call | solution.py:320
  33.3 1.4 %copy.9 = bf16[16,1536]{1,0:T(8,128)(2,1)} copy(bf16[16,1536]{1,0:T(8,128)(2,1)} %shard_map.73) | data formatting | bytes 98304

commit v8 on v7

--- a/solution.py
+++ b/solution.py
@@ -94,6 +94,8 @@
     pl.semaphore_wait(barrier, len(partners))
     tok_load.wait()
 
+    half = depth // 2
+
     def columns(p):
         return pl.ds(p * (width // PARTS), width // PARTS)
 
@@ -135,7 +137,7 @@
         wait_recv(block(zz, ii, jj, p), mark(zz, ii, jj, p))
 
     for p in range(PARTS):
-        for k in range(1, depth):
+        for k in [half] + list(range(1, half)):
             push(z, i, j, p, in_z_send, z_devs[k - 1])
         push(z, i, j, p, in_a_send, a_dev)
         push(z, i, j, p, in_b_send, b_dev)
@@ -147,10 +149,13 @@
         )
         for yy in range(2)
     ]
-    for k in range(1, depth):
+    for k in [half] + list(range(1, half)) + list(range(half + 1, depth)):
         zz = flip(z, k)
         for p in range(PARTS):
             arrived(zz, i, j, p)
+            if k == half:
+                for n in range(1, half):
+                    push(zz, i, j, p, in_z_send, z_devs[n - 1])
             push(zz, i, j, p, in_a_send, a_dev)
             push(zz, i, j, p, in_b_send, b_dev)
     push_sib(i, j, 0, depth)
@@ -186,8 +191,6 @@
             )
             acc[span] = product if first else acc[span] + product
         tiles(one)
-
-    half = depth // 2
 
     def forward(jj, ks, first):
         for k in ks:
@@ -261,7 +264,7 @@
         wait_recv(target.at[slot, :, columns(p)], recv_sem.at[slot * PARTS + p])
         return target[slot, :, columns(p)].astype(F32)
 
-    order = list(range(half, depth)) + list(range(1, half)) + [0]
+    order = list(range(half + 1, depth)) + list(range(1, half)) + [half, 0]
     for yy, jj in ((1 - py, 1 - j), (py, j)):
         down(yy, 1)
         for k in order:
@@ -292,17 +295,25 @@
                 + take(b_r, j * depth + zz, p, b_recv)
                 + take(a_r, zz, p, a_recv)
             )
+            if k == half and half > 1:
+                wait_recv(z_r.at[pl.ds(half, half - 1), :, columns(p)], z_recv.at[PARTS + p])
+                for n in range(half, depth - 1):
+                    value = value + z_r[n, :, columns(p)].astype(F32)
             if k:
-                send(value, z_s, z_r, k - 1, p, z_send, z_recv.at[p], z_devs[k - 1])
+                relay = k > half
+                send(
+                    value, z_s, z_r, k - 1, p, z_send, z_recv.at[PARTS * relay + p],
+                    z_devs[k - half - 1 if relay else k - 1],
+                )
             else:
                 own_part = x[expert, spot(z, px), columns(p)]
                 last.append(value + own_part.astype(F32))
     wait_send(b_s, b_send)
     wait_send(a_s, a_send)
     for p in range(PARTS):
-        wait_recv(z_r.at[:, :, columns(p)], z_recv.at[p])
+        wait_recv(z_r.at[pl.ds(0, half), :, columns(p)], z_recv.at[p])
         value = last[p]
-        for k in range(1, depth):
+        for k in range(1, half + 1):
             value = value + z_r[k - 1, :, columns(p)].astype(F32)
         out[:, columns(p)] = value.astype(BF16)
     wait_send(z_s, z_send)
@@ -346,7 +357,7 @@
             dma((2,)), dma((2,)), dma, dma,
             dma, dma((PARTS * 2 * depth,)),
             dma, dma((PARTS * depth,)),
-            dma, dma((PARTS,)),
+            dma, dma((2 * PARTS,)),
         ],
         compiler_params=pltpu.CompilerParams(
             collective_id=0, has_side_effects=True, vmem_limit_bytes=62 * 1024 * 1024,

time: 34.9 us -> 37.8 us (1.083)
  Pallas kernels: 33.3 us -> 36.2 us
    pallas_call x1, Pallas kernels: 33.3 us -> 36.2 us  [body(): pl.pallas_call(functools.partial(kernel, depth), out_shape=jax.ShapeDtype...]
where the time goes in v8:
time: 37.8 us; the launch traced here: 37.7 us
  Pallas kernels  36.2 us (96%)
  local copies, waits for them, and re-layouts  1.42 us (4%)
    pallas_call x1, Pallas kernels, body(): pl.pallas_call(functools.partial(kernel, depth), out_shape=jax.ShapeDtype...  36.2 us
    unnamed x1, local copies, waits for them, and re-layouts  1.42 us

profile of v8, /device:TPU:0, one launch (start us, length us, event | category | flops | bytes accessed | tf_op | source)
XLA Modules:
  0.0 37.7 jit_solution(2550644632725111080)
XLA Ops:
  0.0 36.2 %shard_map.73 = bf16[16,1536]{1,0:T(8,128)(2,1)} custom-call(bf16[16,1536]{1,0:T(8,128)(2,1)} %tok.1, f32[4,1,1536]{2,1,0:T(1,128)} %bitcast.3, bf16[1,6144,256]{2,1,0:T(8,128)(2,1)} %wg.1, bf16[1,6144,256]{2,1,0:T(8,128)(2,1)} %wu.1, bf16[1,256,6144]{2,1,0:T(8,128)(2,1)} %wd.1, s32[2,128]{1,0:T(2,128)} %bitcast.4, s32[2,128]{1,0:T(2,128)} %bitcast.5), custom_call_target="tpu_custom_call" | custom-call | tf_op jit(solution)/shard_map/pallas_call | solution.py:331
  36.2 1.4 %copy.9 = bf16[16,1536]{1,0:T(8,128)(2,1)} copy(bf16[16,1536]{1,0:T(8,128)(2,1)} %shard_map.73) | data formatting | bytes 98304
